TPU v7x, 256 devices: a whole 4x4x8 slice. The times are simulated.
256 devices in a mesh: seq: 64 (over y, z_lo, x), head: 4 (over z_hi, core).
Axes of the slice: x: 4, y: 4, z: 8 (z_hi: 2, z_lo: 4; z = z_hi * 4 + z_lo), core: 2. Of those that a mesh axis runs over, the one named last changes fastest.
Arguments:
- queries: bfloat16 [16384, 1024], P('seq', 'head'), may hold values from -16 to 16
- key_states: bfloat16 [16384, 1024], P('seq', 'head'), may hold values from -16 to 16
- value_states: bfloat16 [16384, 1024], P('seq', 'head'), may hold values from -6 to 6
- cotangent: bfloat16 [16384, 1024], P('seq', 'head'), may hold values from -6 to 6
- out_weight: bfloat16 [1024, 1024], P('head'), may hold values from -0.1875 to 0.1875
- partner: int32 [64], replicated, may hold values from 0 to 63, as said below
- counts: int32 [64], replicated, may hold values from 128 to 256, as said below
Outputs:
- layer_out: bfloat16 [16384, 1024], P('seq', 'head')
- grad_query: bfloat16 [16384, 1024], P('seq', 'head')
- grad_key: bfloat16 [16384, 1024], P('seq', 'head')
- grad_value: bfloat16 [16384, 1024], P('seq', 'head')
Inputs may be any that keep to these rules, and one draw needn't show every extreme that they name: partner[b] = b XOR r for one r of 1 to 63, the same r for every block; so partner[partner[b]] = b and no block is its own partner. The valid frames of a block are its first counts[b] frames.
All inputs are finite; a program needn't handle non-finite values.
Results may differ from a plain program's by a relative error of at most 0.024.
Values may be sent and summed in bfloat16 or wider, within the bound.
A program may use at most 64 MiB of HBM per device.

v0:
```python
import functools

import jax
import jax.numpy as jnp
from jax import lax
from jax.experimental import pallas as pl
from jax.experimental.pallas import tpu as pltpu
from jax.sharding import PartitionSpec as P

HD = 64
MESH = pl.DeviceIdType.MESH
MASKED = -1e30
BF = jnp.bfloat16
F32 = jnp.float32


def flip(index, offset):
    result = index
    for bit in range(offset.bit_length()):
        if offset >> bit & 1:
            result = result + (1 << bit) * (1 - 2 * ((index // (1 << bit)) % 2))
    return result


def dot(a, b):
    return jnp.dot(a, b, preferred_element_type=F32)


def dot_nt(a, b):
    return lax.dot_general(a, b, (((1,), (1,)), ((), ())), preferred_element_type=F32)


def remote(source, landing, send_sem, recv_sem, target):
    return pltpu.make_async_remote_copy(
        src_ref=source, dst_ref=landing, send_sem=send_sem, recv_sem=recv_sem,
        device_id=target, device_id_type=MESH,
    )


def swap_kernel(
    base, a_ref, b_ref, a_in, b_in, a_relayed, b_relayed, send_sem, recv_sem, relay_send, relay_recv
):
    rows = a_ref.shape[0] // PIECES
    b, h = lax.axis_index("seq"), lax.axis_index("head")
    mate, side = (flip(b, base), h), (flip(b, 1), h)
    barrier = pltpu.get_barrier_semaphore()
    targets = (mate, side) if base else (side,)
    for target in targets:
        pl.semaphore_signal(barrier, inc=1, device_id=target, device_id_type=MESH)
    pl.semaphore_wait(barrier, len(targets))
    direct, relay = [], []
    for array, refs in enumerate(((a_ref, a_in, a_relayed), (b_ref, b_in, b_relayed))):
        for piece in range(PIECES):
            slot = array * PIECES + piece
            source, landing, onward = (ref.at[pl.ds(piece * rows, rows)] for ref in refs)
            if base:
                direct.append(remote(source, landing, send_sem.at[slot], recv_sem.at[slot], mate))
            relay.append(
                remote(
                    landing if base else source, onward, relay_send.at[slot], relay_recv.at[slot],
                    side,
                )
            )
    for copy in direct:
        copy.start()
    for slot, copy in enumerate(relay):
        if base:
            direct[slot].wait_recv()
        copy.start()
    for copy in direct:
        copy.wait_send()
    for copy in relay:
        copy.wait()


def swap(base, first_id, a, b):
    anywhere = pl.BlockSpec(memory_space=pl.ANY)
    shapes = [jax.ShapeDtypeStruct(x.shape, x.dtype) for x in (a, b)]
    return pl.pallas_call(
        functools.partial(swap_kernel, base),
        out_shape=shapes * 2,
        in_specs=[anywhere] * 2,
        out_specs=[anywhere] * 4,
        scratch_shapes=[pltpu.SemaphoreType.DMA((2 * PIECES,))] * 4,
        compiler_params=pltpu.CompilerParams(
            collective_id=first_id + base // 2, has_side_effects=True, vmem_limit_bytes=2 << 20
        ),
    )(a, b)


def swap_any(partner, first_id, a, b):
    pairs = partner.shape[0] // 2
    branches = [
        functools.partial(swap, 2 * pair + pair % 2, first_id) for pair in range(pairs)
    ]
    return lax.switch(partner[0] // 2, branches, a, b)


def choose(partner_ref, direct, relayed):
    offset = partner_ref[0]
    return jnp.where((offset + offset // 2) % 2 == 0, direct[...], relayed[...])


def kernel(
    q_ref, k_ref, v_ref, k_direct, v_direct, k_relayed, v_relayed, cot_ref, w_ref, counts_ref,
    partner_ref, lo_ref, dq_ref, dk_own, dv_own, dk_cross, dv_cross,
    mate_k, mate_v, cots, q_stack, g_stack, k_t, v_t, probs, probs_bf, grads_bf, attn_t, dq_t,
    g_sum, part_own, part_far, part_out, part_in, far_out, far_in, send_sem, recv_sem,
):
    rows, width = q_ref.shape
    heads = width // HD
    b = lax.axis_index("seq")
    h = lax.axis_index("head")
    peer = h + 1 - 2 * (h % 2)
    far = (h + 2) % 4
    far_peer = 3 - h
    to_peer, to_far = (b, peer), (b, far)

    barrier = pltpu.get_barrier_semaphore()
    for target in (to_far, to_peer):
        pl.semaphore_signal(barrier, inc=1, device_id=target, device_id_type=MESH)

    def copy(slot, source, landing, target):
        return remote(source, landing, send_sem.at[slot], recv_sem.at[slot], target)

    def columns(group):
        return pl.ds(pl.multiple_of(group * width, width), width)

    send_cot_far = copy(0, cot_ref, cots.at[0], to_far)
    send_cot_peer = copy(1, cot_ref, cots.at[1], to_peer)
    forward_cot = copy(2, cots.at[0], cots.at[2], to_peer)
    send_part_far = copy(3, part_out.at[0], part_in.at[0], to_peer)
    send_part_peer = copy(4, part_out.at[1], part_in.at[1], to_peer)
    send_far = copy(5, far_out, far_in, to_far)

    mate_k[...] = choose(partner_ref, k_direct, k_relayed)
    mate_v[...] = choose(partner_ref, v_direct, v_relayed)
    lane_head = lax.broadcasted_iota(jnp.int32, (1, width), 1) // HD
    q_scaled = q_ref[...] * jnp.asarray(HD**-0.5, BF)
    for head in range(heads):
        mask = jnp.where(lane_head == head, 1.0, 0.0).astype(BF)
        q_stack[head * rows : (head + 1) * rows, :] = q_scaled * mask
    k_t[:, :rows] = k_ref[...].T
    k_t[:, rows:] = mate_k[...].T
    v_t[:, :rows] = v_ref[...].T
    v_t[:, rows:] = mate_v[...].T
    key_row = lax.broadcasted_iota(jnp.int32, (rows, rows), 0)
    own_valid = key_row < counts_ref[b]
    mate_valid = key_row < counts_ref[partner_ref[b]]

    def head_rows(head):
        return pl.ds(pl.multiple_of(head * rows, rows), rows)

    def forward(head, carry):
        own = jnp.where(own_valid, dot_nt(k_ref[...], q_stack[head_rows(head), :]), MASKED)
        other = jnp.where(mate_valid, dot_nt(mate_k[...], q_stack[head_rows(head), :]), MASKED)
        top = jnp.maximum(
            jnp.max(own, axis=0, keepdims=True), jnp.max(other, axis=0, keepdims=True)
        )
        own = jnp.exp(own - top)
        other = jnp.exp(other - top)
        total = jnp.sum(own, axis=0, keepdims=True) + jnp.sum(other, axis=0, keepdims=True)
        inverse = 1.0 / total
        own = own * inverse
        other = other * inverse
        probs[head, :rows, :] = own
        probs[head, rows:, :] = other
        probs_bf[:rows, head_rows(head)] = own.astype(BF)
        probs_bf[rows:, head_rows(head)] = other.astype(BF)
        lanes = pl.ds(pl.multiple_of(head * HD, HD), HD)
        attn_t[lanes, :] = dot(v_t[lanes, :], probs_bf[:, head_rows(head)]).astype(BF)
        return carry

    lax.fori_loop(0, EARLY, forward, 0)
    pl.semaphore_wait(barrier, 2)
    send_cot_far.start()
    send_cot_peer.start()
    lax.fori_loop(EARLY, heads, forward, 0)

    attention = attn_t[...].T
    part_out[0] = dot(attention, w_ref[:, columns(far_peer)]).astype(BF)
    send_part_far.start()
    part_out[1] = dot(attention, w_ref[:, columns(peer)]).astype(BF)
    send_part_peer.start()
    part_far[...] = dot(attention, w_ref[:, columns(far)])
    part_own[...] = dot(attention, w_ref[:, columns(h)])
    send_part_far.wait_recv()
    far_out[...] = (part_far[...] + part_in[0].astype(F32)).astype(BF)
    send_far.start()
    send_cot_peer.wait_recv()
    g_sum[...] = dot_nt(cot_ref[...], w_ref[:, columns(h)]) + dot_nt(
        cots[1], w_ref[:, columns(peer)]
    )
    send_part_peer.wait_recv()
    part_own[...] += part_in[1].astype(F32)

    send_cot_far.wait_recv()
    forward_cot.start()
    g_sum[...] += dot_nt(cots[0], w_ref[:, columns(far)])
    forward_cot.wait_recv()
    grad_attention = (g_sum[...] + dot_nt(cots[2], w_ref[:, columns(far_peer)])).astype(BF)
    for head in range(heads):
        mask = jnp.where(lane_head == head, 1.0, 0.0).astype(BF)
        g_stack[head * rows : (head + 1) * rows, :] = grad_attention * mask
    products = grad_attention.T.astype(F32) * attn_t[...].astype(F32)
    g_sum[:heads, :] = jnp.sum(products.reshape(heads, HD, rows), axis=1)

    def backward(head, carry):
        delta = g_sum[pl.ds(head, 1), :]
        for half, values in enumerate((v_ref, mate_v)):
            keys = slice(half * rows, (half + 1) * rows)
            grad_probs = dot_nt(values[...], g_stack[head_rows(head), :])
            grads = probs[head, keys, :] * (grad_probs - delta)
            grads_bf[keys, head_rows(head)] = grads.astype(BF)
        lanes = pl.ds(pl.multiple_of(head * HD, HD), HD)
        grads = dot(k_t[lanes, :], grads_bf[:, head_rows(head)])
        dq_t[lanes, :] = (grads * HD**-0.5).astype(BF)
        return carry

    lax.fori_loop(0, heads, backward, 0)
    dq_ref[...] = dq_t[...].T
    dv_cross[...] = dot(probs_bf[rows:, :], g_stack[...]).astype(BF)
    dk_cross[...] = dot(grads_bf[rows:, :], q_stack[...]).astype(BF)
    dv_own[...] = dot(probs_bf[:rows, :], g_stack[...])
    dk_own[...] = dot(grads_bf[:rows, :], q_stack[...])

    send_far.wait_recv()
    lo_ref[...] = (part_own[...] + far_in[...].astype(F32)).astype(BF)
    for sent in (
        send_cot_far, send_cot_peer, forward_cot, send_part_far, send_part_peer, send_far,
    ):
        sent.wait_send()


def attend(queries, key_states, value_states, mates, cotangent, out_weight, counts, partner):
    rows, width = queries.shape
    heads = width // HD
    narrow = jax.ShapeDtypeStruct((rows, width), BF)
    wide = jax.ShapeDtypeStruct((rows, width), F32)
    vmem = pl.BlockSpec(memory_space=pltpu.VMEM)
    smem = pl.BlockSpec(memory_space=pltpu.SMEM)
    scratch = [
        pltpu.VMEM((rows, width), BF),
        pltpu.VMEM((rows, width), BF),
        pltpu.VMEM((3, rows, width), BF),
        pltpu.VMEM((heads * rows, width), BF),
        pltpu.VMEM((heads * rows, width), BF),
        pltpu.VMEM((width, 2 * rows), BF),
        pltpu.VMEM((width, 2 * rows), BF),
        pltpu.VMEM((heads, 2 * rows, rows), F32),
        pltpu.VMEM((2 * rows, heads * rows), BF),
        pltpu.VMEM((2 * rows, heads * rows), BF),
        pltpu.VMEM((width, rows), BF),
        pltpu.VMEM((width, rows), BF),
        pltpu.VMEM((rows, width), F32),
        pltpu.VMEM((rows, width), F32),
        pltpu.VMEM((rows, width), F32),
        pltpu.VMEM((2, rows, width), BF),
        pltpu.VMEM((2, rows, width), BF),
        pltpu.VMEM((rows, width), BF),
        pltpu.VMEM((rows, width), BF),
        pltpu.SemaphoreType.DMA((6,)),
        pltpu.SemaphoreType.DMA((6,)),
    ]
    return pl.pallas_call(
        kernel,
        out_shape=(narrow, narrow, wide, wide, narrow, narrow),
        in_specs=[vmem] * 9 + [smem] * 2,
        out_specs=(vmem,) * 6,
        scratch_shapes=scratch,
        compiler_params=pltpu.CompilerParams(
            collective_id=0, has_side_effects=True, vmem_limit_bytes=20 << 20
        ),
        cost_estimate=pl.CostEstimate(
            flops=600_000_000, bytes_accessed=3 << 20, transcendentals=524288
        ),
    )(queries, key_states, value_states, *mates, cotangent, out_weight, counts, partner)


def finish_kernel(
    lo, dq, dk_own, dv_own, dk_direct, dv_direct, dk_relayed, dv_relayed, partner_ref,
    lo_ref, dq_ref, dk_ref, dv_ref,
):
    lo_ref[...] = lo[...]
    dq_ref[...] = dq[...]
    dk_ref[...] = (dk_own[...] + choose(partner_ref, dk_direct, dk_relayed).astype(F32)).astype(BF)
    dv_ref[...] = (dv_own[...] + choose(partner_ref, dv_direct, dv_relayed).astype(F32)).astype(BF)


def finish(lo, dq, dk_own, dv_own, returned, partner):
    vmem = pl.BlockSpec(memory_space=pltpu.VMEM)
    smem = pl.BlockSpec(memory_space=pltpu.SMEM)
    return pl.pallas_call(
        finish_kernel,
        out_shape=(jax.ShapeDtypeStruct(lo.shape, BF),) * 4,
        in_specs=[vmem] * 8 + [smem],
        out_specs=(vmem,) * 4,
        compiler_params=pltpu.CompilerParams(vmem_limit_bytes=4 << 20),
    )(lo, dq, dk_own, dv_own, *returned, partner)


EARLY = 2
PIECES = 2


def per_device(queries, key_states, value_states, cotangent, out_weight, partner, counts):
    mates = swap_any(partner, 1, key_states, value_states)
    lo, dq, dk_own, dv_own, dk_cross, dv_cross = attend(
        queries, key_states, value_states, mates, cotangent, out_weight, counts, partner
    )
    returned = swap_any(partner, 1, dk_cross, dv_cross)
    return finish(lo, dq, dk_own, dv_own, returned, partner)


def solution(mesh):
    return jax.shard_map(
        per_device,
        mesh=mesh,
        in_specs=(
            P("seq", "head"), P("seq", "head"), P("seq", "head"), P("seq", "head"),
            P("head", None), P(), P(),
        ),
        out_specs=(P("seq", "head"),) * 4,
        check_vma=False,
    )
```

profile of v0, /device:TPU:32, one launch (start us, length us, event | category | flops | bytes accessed | tf_op | source)
XLA Modules:
  0.0 51.2 jit_solution(18168929362881532506)
XLA Ops:
  0.6 0.0 copy-start
  0.6 0.6 %copy-done = s32[64]{0:T(128)S(1)} copy-done((s32[64]{0:T(128)S(1)}, s32[64]{0:T(128)}, u32[]{:S(2)}) %copy-start) | copy-done | bytes 280
  1.5 0.0 copy-start.1
  1.5 0.0 copy-start.2
  1.5 0.0 copy-start.3
  1.5 13.4 %conditional.2 = ((bf16[256,256]{1,0:T(8,128)(2,1)S(1)}, bf16[256,256]{1,0:T(8,128)(2,1)S(1)}, bf16[256,256]{1,0:T(8,128)(2,1)S(1)}, bf16[256,256]{1,0:T(8,128)(2,1)S(1)})) conditional(s32[]{:T(128)} %clamp.4, (bf16[256,256]{1,0:T(8,128)(2,1)}, bf16[256,256]{1,0:T(8,128)(2,1)}) %tuple.199, ...), branch_computations={%region_0.1_spmd, %region_1.2_spmd, %region_2.3_spmd, %region_3.4_... | conditional | bytes 8 | solution.py:96
  1.5 13.3 %branch_1_fun.2 = (bf16[256,256]{1,0:T(8,128)(2,1)S(1)}, bf16[256,256]{1,0:T(8,128)(2,1)S(1)}, bf16[256,256]{1,0:T(8,128)(2,1)S(1)}, bf16[256,256]{1,0:T(8,128)(2,1)S(1)}) custom-call(bf16[256,256]{1,0:T(8,128)(2,1)} %get-tuple-element.258.a_ref, bf16[256,256]{1,0:T(8,128)(2,1)} %get-tuple-element.259.b_ref), custom_call_target="tpu_custom_call" | custom-call | tf_op jit(solution)/shard_map/cond/branch_1_fun/pallas_call | solution.py:79
  14.9 0.0 copy-start.4
  14.9 0.0 copy-done.1
  14.9 0.0 copy-done.2
  14.9 0.0 copy-done.3
  14.9 0.6 %copy-done.4 = s32[64]{0:T(128)S(1)} copy-done((s32[64]{0:T(128)S(1)}, s32[64]{0:T(128)}, u32[]{:S(2)}) %copy-start.4) | copy-done | bytes 280
  15.6 20.5 %shard_map.102 = (bf16[256,256]{1,0:T(8,128)(2,1)S(1)}, bf16[256,256]{1,0:T(8,128)(2,1)S(1)}, f32[256,256]{1,0:T(8,128)S(1)}, f32[256,256]{1,0:T(8,128)S(1)}, bf...) custom-call(bf16[256,256]{1,0:T(8,128)(2,1)S(1)} %copy-done.2, bf16[256,256]{1,0:T(8,128)(2,1)} %k_ref.1, ...), custom_call_target="tpu_custom_call" | custom-call | flops 600000000 | bytes 3145728 | tf_op jit(solution)/shard_map/pallas_call | solution.py:265
  36.1 13.7 %conditional.3 = ((bf16[256,256]{1,0:T(8,128)(2,1)S(1)}, bf16[256,256]{1,0:T(8,128)(2,1)S(1)}, bf16[256,256]{1,0:T(8,128)(2,1)S(1)}, bf16[256,256]{1,0:T(8,128)(2,1)S(1)})) conditional(s32[]{:T(128)} %clamp.4, (bf16[256,256]{1,0:T(8,128)(2,1)S(1)}, bf16[256,256]{1,0:T(8,128)(2,1)S(1)}) %tuple.200, ...), branch_computations={%region_32.33_spmd, %region_33.34_spmd, %region_34.35_spmd, %regio... | conditional | bytes 8 | solution.py:96
  36.1 13.5 %branch_1_fun.3 = (bf16[256,256]{1,0:T(8,128)(2,1)S(1)}, bf16[256,256]{1,0:T(8,128)(2,1)S(1)}, bf16[256,256]{1,0:T(8,128)(2,1)S(1)}, bf16[256,256]{1,0:T(8,128)(2,1)S(1)}) custom-call(bf16[256,256]{1,0:T(8,128)(2,1)S(1)} %get-tuple-element.322.a_ref, bf16[256,256]{1,0:T(8,128)(2,1)S(1)} %get-tuple-element.323.b_ref), custom_call_target="tpu_custom_call" | custom-call | tf_op jit(solution)/shard_map/cond/branch_1_fun/pallas_call | solution.py:79
  49.8 1.4 %shard_map.103 = (bf16[256,256]{1,0:T(8,128)(2,1)}, bf16[256,256]{1,0:T(8,128)(2,1)}, bf16[256,256]{1,0:T(8,128)(2,1)}, bf16[256,256]{1,0:T(8,128)(2,1)}) custom-call(bf16[256,256]{1,0:T(8,128)(2,1)S(1)} %get-tuple-element.406.lo, bf16[256,256]{1,0:T(8,128)(2,1)S(1)} %get-tuple-element.407.dq, f32[256,256]{1,0:T(8,128)S(1)} %get-tuple-element.408.dk_own, ...), custom_call_target="tpu_custom_call" | custom-call | tf_op jit(solution)/shard_map/pallas_call | solution.py:293
Async XLA Ops:
  0.6 0.7 %copy-start = (s32[64]{0:T(128)S(1)}, s32[64]{0:T(128)}, u32[]{:S(2)}) copy-start(s32[64]{0:T(128)} %partner_ref.3) | copy-start | bytes 772
  1.5 13.5 %copy-start.1 = (bf16[256,1024]{1,0:T(8,128)(2,1)S(1)}, bf16[256,1024]{1,0:T(8,128)(2,1)}, u32[]{:S(2)}) copy-start(bf16[256,1024]{1,0:T(8,128)(2,1)} %w_ref.1) | copy-start | bytes 1572868
  1.5 13.5 %copy-start.2 = (bf16[256,256]{1,0:T(8,128)(2,1)S(1)}, bf16[256,256]{1,0:T(8,128)(2,1)}, u32[]{:S(2)}) copy-start(bf16[256,256]{1,0:T(8,128)(2,1)} %q_ref.1) | copy-start | bytes 393220
  1.5 13.5 %copy-start.3 = (bf16[256,256]{1,0:T(8,128)(2,1)S(1)}, bf16[256,256]{1,0:T(8,128)(2,1)}, u32[]{:S(2)}) copy-start(bf16[256,256]{1,0:T(8,128)(2,1)} %cot_ref.1) | copy-start | bytes 393220
  14.9 0.7 %copy-start.4 = (s32[64]{0:T(128)S(1)}, s32[64]{0:T(128)}, u32[]{:S(2)}) copy-start(s32[64]{0:T(128)} %counts_ref.1) | copy-start | bytes 772
where the time goes:
time: 52.2 us; the launch traced here: 51.2 us
  Pallas kernels  48.7 us (93%)
  local copies, waits for them, and re-layouts  1.28 us (2%)
  between operations  0.88 us (2%)
    pallas_call x2, Pallas kernels, swap(): pl.pallas_call(functools.partial(swap_kernel, base), out_shape=shapes * 2...  26.8 us
    pallas_call x1, Pallas kernels, attend(): pl.pallas_call(kernel, out_shape=(narrow, narrow, wide, wide, narrow, nar...  20.5 us
    pallas_call x1, Pallas kernels, finish(): pl.pallas_call(finish_kernel, out_shape=(jax.ShapeDtypeStruct(lo.shape, B...  1.39 us
    unnamed x10, local copies, waits for them, and re-layouts  1.28 us

commit v1 on v0

--- a/solution.py
+++ b/solution.py
@@ -38,54 +38,78 @@
 
 
 def swap_kernel(
-    base, a_ref, b_ref, a_in, b_in, a_relayed, b_relayed, send_sem, recv_sem, relay_send, relay_recv
+    base, a_ref, b_ref, partner_ref, a_in, a_relayed, b_in, b_own, b_side, b_pick, partner,
+    load_sem, a_send, a_recv, relay_send, relay_recv, side_send, side_recv, b_send, b_recv,
 ):
     rows = a_ref.shape[0] // PIECES
     b, h = lax.axis_index("seq"), lax.axis_index("head")
     mate, side = (flip(b, base), h), (flip(b, 1), h)
+    targets = (mate, side) if base else (side,)
+    load_b = pltpu.make_async_copy(b_ref, b_own, load_sem.at[0])
+    load_partner = pltpu.make_async_copy(partner_ref, partner, load_sem.at[1])
+    if base:
+        load_b.start()
+        load_partner.start()
     barrier = pltpu.get_barrier_semaphore()
-    targets = (mate, side) if base else (side,)
     for target in targets:
         pl.semaphore_signal(barrier, inc=1, device_id=target, device_id_type=MESH)
     pl.semaphore_wait(barrier, len(targets))
-    direct, relay = [], []
-    for array, refs in enumerate(((a_ref, a_in, a_relayed), (b_ref, b_in, b_relayed))):
-        for piece in range(PIECES):
-            slot = array * PIECES + piece
-            source, landing, onward = (ref.at[pl.ds(piece * rows, rows)] for ref in refs)
-            if base:
-                direct.append(remote(source, landing, send_sem.at[slot], recv_sem.at[slot], mate))
-            relay.append(
-                remote(
-                    landing if base else source, onward, relay_send.at[slot], relay_recv.at[slot],
-                    side,
-                )
+
+    def pieces(source, landing, send_sem, recv_sem, target):
+        return [
+            remote(
+                source.at[pl.ds(i * rows, rows)], landing.at[pl.ds(i * rows, rows)],
+                send_sem.at[i], recv_sem.at[i], target,
             )
-    for copy in direct:
+            for i in range(PIECES)
+        ]
+
+    relay_a = pieces(a_in if base else a_ref, a_relayed, relay_send, relay_recv, side)
+    side_b = pieces(b_ref, b_side if base else b_in, side_send, side_recv, side)
+    for copy in side_b:
         copy.start()
-    for slot, copy in enumerate(relay):
-        if base:
-            direct[slot].wait_recv()
+    if not base:
+        for copy in relay_a:
+            copy.start()
+        for copy in side_b + relay_a:
+            copy.wait()
+        return
+    direct_a = pieces(a_ref, a_in, a_send, a_recv, mate)
+    picked_b = pieces(b_pick, b_in, b_send, b_recv, mate)
+    for copy in direct_a:
         copy.start()
-    for copy in direct:
+    load_b.wait()
+    load_partner.wait()
+    relayed = is_relayed(partner)
+    for i in range(PIECES):
+        side_b[i].wait_recv()
+        piece = slice(i * rows, (i + 1) * rows)
+        b_pick[piece, :] = jnp.where(relayed, b_side[piece, :], b_own[piece, :])
+        picked_b[i].start()
+    for i in range(PIECES):
+        direct_a[i].wait_recv()
+        relay_a[i].start()
+    for copy in side_b + direct_a:
         copy.wait_send()
-    for copy in relay:
+    for copy in picked_b + relay_a:
         copy.wait()
 
 
-def swap(base, first_id, a, b):
+def swap(base, first_id, a, b, partner):
     anywhere = pl.BlockSpec(memory_space=pl.ANY)
-    shapes = [jax.ShapeDtypeStruct(x.shape, x.dtype) for x in (a, b)]
+    shapes = [jax.ShapeDtypeStruct(x.shape, x.dtype) for x in (a, a, b)]
     return pl.pallas_call(
         functools.partial(swap_kernel, base),
-        out_shape=shapes * 2,
-        in_specs=[anywhere] * 2,
-        out_specs=[anywhere] * 4,
-        scratch_shapes=[pltpu.SemaphoreType.DMA((2 * PIECES,))] * 4,
+        out_shape=shapes,
+        in_specs=[anywhere] * 3,
+        out_specs=[anywhere] * 3,
+        scratch_shapes=[pltpu.VMEM(b.shape, b.dtype)] * 3
+        + [pltpu.SMEM(partner.shape, partner.dtype), pltpu.SemaphoreType.DMA((2,))]
+        + [pltpu.SemaphoreType.DMA((PIECES,))] * 8,
         compiler_params=pltpu.CompilerParams(
             collective_id=first_id + base // 2, has_side_effects=True, vmem_limit_bytes=2 << 20
         ),
-    )(a, b)
+    )(a, b, partner)
 
 
 def swap_any(partner, first_id, a, b):
@@ -93,18 +117,22 @@
     branches = [
         functools.partial(swap, 2 * pair + pair % 2, first_id) for pair in range(pairs)
     ]
-    return lax.switch(partner[0] // 2, branches, a, b)
+    return lax.switch(partner[0] // 2, branches, a, b, partner)
+
+
+def is_relayed(partner_ref):
+    offset = partner_ref[0]
+    return (offset + offset // 2) % 2 == 1
 
 
 def choose(partner_ref, direct, relayed):
-    offset = partner_ref[0]
-    return jnp.where((offset + offset // 2) % 2 == 0, direct[...], relayed[...])
+    return jnp.where(is_relayed(partner_ref), relayed[...], direct[...])
 
 
 def kernel(
-    q_ref, k_ref, v_ref, k_direct, v_direct, k_relayed, v_relayed, cot_ref, w_ref, counts_ref,
+    q_ref, k_ref, v_ref, k_direct, k_relayed, mate_v, cot_ref, w_ref, counts_ref,
     partner_ref, lo_ref, dq_ref, dk_own, dv_own, dk_cross, dv_cross,
-    mate_k, mate_v, cots, q_stack, g_stack, k_t, v_t, probs, probs_bf, grads_bf, attn_t, dq_t,
+    mate_k, cots, q_stack, g_stack, k_t, v_t, probs, probs_bf, grads_bf, attn_t, dq_t,
     g_sum, part_own, part_far, part_out, part_in, far_out, far_in, send_sem, recv_sem,
 ):
     rows, width = q_ref.shape
@@ -134,7 +162,6 @@
     send_far = copy(5, far_out, far_in, to_far)
 
     mate_k[...] = choose(partner_ref, k_direct, k_relayed)
-    mate_v[...] = choose(partner_ref, v_direct, v_relayed)
     lane_head = lax.broadcasted_iota(jnp.int32, (1, width), 1) // HD
     q_scaled = q_ref[...] * jnp.asarray(HD**-0.5, BF)
     for head in range(heads):
@@ -240,7 +267,6 @@
     vmem = pl.BlockSpec(memory_space=pltpu.VMEM)
     smem = pl.BlockSpec(memory_space=pltpu.SMEM)
     scratch = [
-        pltpu.VMEM((rows, width), BF),
         pltpu.VMEM((rows, width), BF),
         pltpu.VMEM((3, rows, width), BF),
         pltpu.VMEM((heads * rows, width), BF),
@@ -265,7 +291,7 @@
     return pl.pallas_call(
         kernel,
         out_shape=(narrow, narrow, wide, wide, narrow, narrow),
-        in_specs=[vmem] * 9 + [smem] * 2,
+        in_specs=[vmem] * 8 + [smem] * 2,
         out_specs=(vmem,) * 6,
         scratch_shapes=scratch,
         compiler_params=pltpu.CompilerParams(
@@ -278,13 +304,13 @@
 
 
 def finish_kernel(
-    lo, dq, dk_own, dv_own, dk_direct, dv_direct, dk_relayed, dv_relayed, partner_ref,
+    lo, dq, dk_own, dv_own, dk_direct, dk_relayed, dv_in, partner_ref,
     lo_ref, dq_ref, dk_ref, dv_ref,
 ):
     lo_ref[...] = lo[...]
     dq_ref[...] = dq[...]
     dk_ref[...] = (dk_own[...] + choose(partner_ref, dk_direct, dk_relayed).astype(F32)).astype(BF)
-    dv_ref[...] = (dv_own[...] + choose(partner_ref, dv_direct, dv_relayed).astype(F32)).astype(BF)
+    dv_ref[...] = (dv_own[...] + dv_in[...].astype(F32)).astype(BF)
 
 
 def finish(lo, dq, dk_own, dv_own, returned, partner):
@@ -293,14 +319,14 @@
     return pl.pallas_call(
         finish_kernel,
         out_shape=(jax.ShapeDtypeStruct(lo.shape, BF),) * 4,
-        in_specs=[vmem] * 8 + [smem],
+        in_specs=[vmem] * 7 + [smem],
         out_specs=(vmem,) * 4,
         compiler_params=pltpu.CompilerParams(vmem_limit_bytes=4 << 20),
     )(lo, dq, dk_own, dv_own, *returned, partner)
 
 
 EARLY = 2
-PIECES = 2
+PIECES = 4
 
 
 def per_device(queries, key_states, value_states, cotangent, out_weight, partner, counts):

time: 52.2 us -> 52.3 us (level); the launches traced: 51.2 us -> 52.2 us
  Pallas kernels: 48.7 us -> 49.4 us
    pallas_call x2, Pallas kernels: 26.8 us -> 30.2 us  [swap(): pl.pallas_call(functools.partial(swap_kernel, base), out_shape=shapes, in...]
    pallas_call x1, Pallas kernels: 20.5 us -> 17.8 us  [attend(): pl.pallas_call(kernel, out_shape=(narrow, narrow, wide, wide, narrow, nar...]
where the time goes in v1:
time: 52.3 us; the launch traced here: 52.2 us
  Pallas kernels  49.4 us (94%)
  local copies, waits for them, and re-layouts  1.28 us (2%)
  between operations  0.88 us (2%)
  loops' own time  0.59 us (1%)
    pallas_call x2, Pallas kernels, swap(): pl.pallas_call(functools.partial(swap_kernel, base), out_shape=shapes, in...  30.2 us
    pallas_call x1, Pallas kernels, attend(): pl.pallas_call(kernel, out_shape=(narrow, narrow, wide, wide, narrow, nar...  17.8 us
    pallas_call x1, Pallas kernels, finish(): pl.pallas_call(finish_kernel, out_shape=(jax.ShapeDtypeStruct(lo.shape, B...  1.37 us
    unnamed x10, local copies, waits for them, and re-layouts  1.28 us

profile of v1, /device:TPU:32, one launch (start us, length us, event | category | flops | bytes accessed | tf_op | source)
XLA Modules:
  0.0 52.2 jit_solution(9647306959738801159)
XLA Ops:
  0.6 0.0 copy-start.4
  0.6 0.6 %copy-done.4 = s32[64]{0:T(128)S(1)} copy-done((s32[64]{0:T(128)S(1)}, s32[64]{0:T(128)}, u32[]{:S(2)}) %copy-start.4) | copy-done | bytes 280
  1.5 0.0 copy-start
  1.5 0.0 copy-start.1
  1.5 0.0 copy-start.2
  1.5 17.8 %conditional.2 = ((bf16[256,256]{1,0:T(8,128)(2,1)S(1)}, bf16[256,256]{1,0:T(8,128)(2,1)S(1)}, bf16[256,256]{1,0:T(8,128)(2,1)S(1)})) conditional(s32[]{:T(128)} %clamp.4, (bf16[256,256]{1,0:T(8,128)(2,1)}, bf16[256,256]{1,0:T(8,128)(2,1)}, s32[64]{0:T(128)S(1)}) %tuple.359, (bf16[256,256]{1,0:T(8,128)(2,1)}, ...), branch_computations={%region_0.1_spmd, %region_1.2_spmd, %region_2.3_spmd, %region_3.4_... | conditional | bytes 8 | solution.py:120
  1.5 17.5 %branch_14_fun.2 = (bf16[256,256]{1,0:T(8,128)(2,1)S(1)}, bf16[256,256]{1,0:T(8,128)(2,1)S(1)}, bf16[256,256]{1,0:T(8,128)(2,1)S(1)}) custom-call(bf16[256,256]{1,0:T(8,128)(2,1)} %get-tuple-element.426.a_ref, bf16[256,256]{1,0:T(8,128)(2,1)} %get-tuple-element.427.b_ref, s32[64]{0:T(128)S(1)} %get-tuple-element.428.partner_ref), custom_call_target="tpu_custom_call" | custom-call | tf_op jit(solution)/shard_map/cond/branch_14_fun/pallas_call | solution.py:101
  19.3 0.0 copy-start.3
  19.3 0.0 copy-done
  19.3 0.0 copy-done.1
  19.3 0.0 copy-done.2
  19.3 0.6 %copy-done.3 = s32[64]{0:T(128)S(1)} copy-done((s32[64]{0:T(128)S(1)}, s32[64]{0:T(128)}, u32[]{:S(2)}) %copy-start.3) | copy-done | bytes 280
  19.9 17.8 %shard_map.102 = (bf16[256,256]{1,0:T(8,128)(2,1)S(1)}, bf16[256,256]{1,0:T(8,128)(2,1)S(1)}, f32[256,256]{1,0:T(8,128)S(1)}, f32[256,256]{1,0:T(8,128)S(1)}, bf...) custom-call(bf16[256,256]{1,0:T(8,128)(2,1)S(1)} %copy-done.1, bf16[256,256]{1,0:T(8,128)(2,1)} %k_ref.1, ...), custom_call_target="tpu_custom_call" | custom-call | flops 600000000 | bytes 3145728 | tf_op jit(solution)/shard_map/pallas_call | solution.py:291
  37.8 13.0 %conditional.3 = ((bf16[256,256]{1,0:T(8,128)(2,1)S(1)}, bf16[256,256]{1,0:T(8,128)(2,1)S(1)}, bf16[256,256]{1,0:T(8,128)(2,1)S(1)})) conditional(s32[]{:T(128)} %clamp.4, (bf16[256,256]{1,0:T(8,128)(2,1)S(1)}, bf16[256,256]{1,0:T(8,128)(2,1)S(1)}, s32[64]{0:T(128)S(1)}) %tuple.361, (bf16[256,256]{1,0:T(8,128)(2,1)S(1)}, ...), branch_computations={%region_32.33_spmd, %region_33.34_spmd, %region_34.35_spmd, %regio... | conditional | bytes 8 | solution.py:120
  37.8 12.7 %branch_14_fun.3 = (bf16[256,256]{1,0:T(8,128)(2,1)S(1)}, bf16[256,256]{1,0:T(8,128)(2,1)S(1)}, bf16[256,256]{1,0:T(8,128)(2,1)S(1)}) custom-call(bf16[256,256]{1,0:T(8,128)(2,1)S(1)} %get-tuple-element.522.a_ref, bf16[256,256]{1,0:T(8,128)(2,1)S(1)} %get-tuple-element.523.b_ref, s32[64]{0:T(128)S(1)} %get-tuple-element.524.partner_ref), custom_call_target="tpu_custom_call" | custom-call | tf_op jit(solution)/shard_map/cond/branch_14_fun/pallas_call | solution.py:101
  50.8 1.4 %shard_map.103 = (bf16[256,256]{1,0:T(8,128)(2,1)}, bf16[256,256]{1,0:T(8,128)(2,1)}, bf16[256,256]{1,0:T(8,128)(2,1)}, bf16[256,256]{1,0:T(8,128)(2,1)}) custom-call(bf16[256,256]{1,0:T(8,128)(2,1)S(1)} %get-tuple-element.595.lo, bf16[256,256]{1,0:T(8,128)(2,1)S(1)} %get-tuple-element.596.dq, f32[256,256]{1,0:T(8,128)S(1)} %get-tuple-element.597.dk_own, ...), custom_call_target="tpu_custom_call" | custom-call | tf_op jit(solution)/shard_map/pallas_call | solution.py:319
Async XLA Ops:
  0.6 0.7 %copy-start.4 = (s32[64]{0:T(128)S(1)}, s32[64]{0:T(128)}, u32[]{:S(2)}) copy-start(s32[64]{0:T(128)} %partner_ref.3) | copy-start | bytes 772
  1.5 17.8 %copy-start = (bf16[256,1024]{1,0:T(8,128)(2,1)S(1)}, bf16[256,1024]{1,0:T(8,128)(2,1)}, u32[]{:S(2)}) copy-start(bf16[256,1024]{1,0:T(8,128)(2,1)} %w_ref.1) | copy-start | bytes 1572868
  1.5 17.8 %copy-start.1 = (bf16[256,256]{1,0:T(8,128)(2,1)S(1)}, bf16[256,256]{1,0:T(8,128)(2,1)}, u32[]{:S(2)}) copy-start(bf16[256,256]{1,0:T(8,128)(2,1)} %q_ref.1) | copy-start | bytes 393220
  1.5 17.8 %copy-start.2 = (bf16[256,256]{1,0:T(8,128)(2,1)S(1)}, bf16[256,256]{1,0:T(8,128)(2,1)}, u32[]{:S(2)}) copy-start(bf16[256,256]{1,0:T(8,128)(2,1)} %cot_ref.1) | copy-start | bytes 393220
  19.3 0.7 %copy-start.3 = (s32[64]{0:T(128)S(1)}, s32[64]{0:T(128)}, u32[]{:S(2)}) copy-start(s32[64]{0:T(128)} %counts_ref.1) | copy-start | bytes 772

commit v2 on v1

v2 whole, which is shorter than its diff:
```python
import functools

import jax
import jax.numpy as jnp
from jax import lax
from jax.experimental import pallas as pl
from jax.experimental.pallas import tpu as pltpu
from jax.sharding import PartitionSpec as P

HD = 64
MESH = pl.DeviceIdType.MESH
MASKED = -1e30
BF = jnp.bfloat16
F32 = jnp.float32


def flip(index, offset):
    result = index
    for bit in range(offset.bit_length()):
        if offset >> bit & 1:
            result = result + (1 << bit) * (1 - 2 * ((index // (1 << bit)) % 2))
    return result


def dot(a, b):
    return jnp.dot(a, b, preferred_element_type=F32)


def dot_nt(a, b):
    return lax.dot_general(a, b, (((1,), (1,)), ((), ())), preferred_element_type=F32)


def remote(source, landing, send_sem, recv_sem, target):
    return pltpu.make_async_remote_copy(
        src_ref=source, dst_ref=landing, send_sem=send_sem, recv_sem=recv_sem,
        device_id=target, device_id_type=MESH,
    )


def swap_kernel(base, inputs, outputs, scratch):
    a_ref, b_ref, *c_ref, partner_ref = inputs
    a_in, a_relayed, b_in, *c_in = outputs
    (
        b_own, b_side, b_pick, partner, load_sem, a_send, a_recv, relay_send, relay_recv,
        side_send, side_recv, b_send, b_recv, c_sem,
    ) = scratch
    rows = a_ref.shape[0] // PIECES
    b, h = lax.axis_index("seq"), lax.axis_index("head")
    mate, side = (flip(b, base), h), (flip(b, 1), h)
    far = (b, (h + 2) % 4)
    targets = [side] + [mate] * bool(base) + [far] * len(c_ref)
    load_b = pltpu.make_async_copy(b_ref, b_own, load_sem.at[0])
    load_partner = pltpu.make_async_copy(partner_ref, partner, load_sem.at[1])
    if base:
        load_b.start()
        load_partner.start()
    barrier = pltpu.get_barrier_semaphore()
    for target in targets:
        pl.semaphore_signal(barrier, inc=1, device_id=target, device_id_type=MESH)
    pl.semaphore_wait(barrier, len(targets))

    def pieces(source, landing, send_sem, recv_sem, target):
        return [
            remote(
                source.at[pl.ds(i * rows, rows)], landing.at[pl.ds(i * rows, rows)],
                send_sem.at[i], recv_sem.at[i], target,
            )
            for i in range(PIECES)
        ]

    relay_a = pieces(a_in if base else a_ref, a_relayed, relay_send, relay_recv, side)
    side_b = pieces(b_ref, b_side if base else b_in, side_send, side_recv, side)
    sent_c = [remote(c_ref[0], c_in[0], c_sem.at[0], c_sem.at[1], far)] if c_ref else []
    for copy in sent_c:
        copy.start()
    for copy in side_b:
        copy.start()
    if not base:
        for copy in relay_a:
            copy.start()
        for copy in side_b + relay_a + sent_c:
            copy.wait()
        return
    direct_a = pieces(a_ref, a_in, a_send, a_recv, mate)
    picked_b = pieces(b_pick, b_in, b_send, b_recv, mate)
    for copy in direct_a:
        copy.start()
    load_b.wait()
    load_partner.wait()
    relayed = is_relayed(partner)
    for i in range(PIECES):
        side_b[i].wait_recv()
        piece = slice(i * rows, (i + 1) * rows)
        b_pick[piece, :] = jnp.where(relayed, b_side[piece, :], b_own[piece, :])
        picked_b[i].start()
    for i in range(PIECES):
        direct_a[i].wait_recv()
        relay_a[i].start()
    for copy in side_b + direct_a:
        copy.wait_send()
    for copy in picked_b + relay_a + sent_c:
        copy.wait()


def swap(base, arrays, partner):
    anywhere = pl.BlockSpec(memory_space=pl.ANY)
    shapes = [jax.ShapeDtypeStruct(x.shape, x.dtype) for x in (arrays[0], *arrays)]
    block = pltpu.VMEM(arrays[1].shape, arrays[1].dtype)
    taken, given = len(arrays) + 1, len(shapes)

    def body(*refs):
        swap_kernel(base, refs[:taken], refs[taken : taken + given], refs[taken + given :])

    return pl.pallas_call(
        body,
        out_shape=shapes,
        in_specs=[anywhere] * taken,
        out_specs=[anywhere] * given,
        scratch_shapes=[block] * 3
        + [pltpu.SMEM(partner.shape, partner.dtype), pltpu.SemaphoreType.DMA((2,))]
        + [pltpu.SemaphoreType.DMA((PIECES,))] * 8
        + [pltpu.SemaphoreType.DMA((2,))],
        compiler_params=pltpu.CompilerParams(
            collective_id=2 + base // 2, has_side_effects=True, vmem_limit_bytes=2 << 20
        ),
    )(*arrays, partner)


def swap_any(pairs, which, arrays, partner):
    branches = [
        functools.partial(lambda base, *args: swap(base, args[:-1], args[-1]), 2 * pair + pair % 2)
        for pair in pairs
    ]
    return lax.switch(which, branches, *arrays, partner)


def is_relayed(partner_ref):
    offset = partner_ref[0]
    return (offset + offset // 2) % 2 == 1


def choose(partner_ref, direct, relayed):
    return jnp.where(is_relayed(partner_ref), relayed[...], direct[...])


def kernel(inside, inputs, outputs, scratch):
    if inside:
        q_any, k_any, v_any, k_direct, k_relayed, mate_v, cot_any, w_any, counts_any, partner_any = inputs
        part_own, far_in, dq_ref, dk_own, dv_own, dk_cross, dv_cross = outputs
    else:
        (
            q_any, k_any, v_any, k_direct, k_relayed, mate_v, cot_any, w_any, counts_any, partner_any,
            cot_far,
        ) = inputs
        part_own, far_out, dq_ref, dk_own, dv_own, dk_cross, dv_cross = outputs
    (
        q_ref, k_ref, v_ref, cot_ref, w_ref, counts_ref, partner_ref, mate_k, cots, q_stack, g_stack, k_t, v_t, probs, probs_bf,
        grads_bf, attn_t, dq_t, delta, g_sum, part_far, part_out, part_in, load_sem, send_sem, recv_sem,
        *spare,
    ) = scratch
    if inside:
        cot_far, far_out = spare
    rows, width = q_ref.shape
    heads = width // HD
    b = lax.axis_index("seq")
    h = lax.axis_index("head")
    peer = h + 1 - 2 * (h % 2)
    far = (h + 2) % 4
    far_peer = 3 - h
    to_peer, to_far = (b, peer), (b, far)

    barrier = pltpu.get_barrier_semaphore()
    targets = (to_far, to_peer) if inside else (to_peer,)
    for target in targets:
        pl.semaphore_signal(barrier, inc=1, device_id=target, device_id_type=MESH)
    loads = [
        pltpu.make_async_copy(source, landing, load_sem.at[i])
        for i, (source, landing) in enumerate(
            (
                (q_any, q_ref), (partner_any, partner_ref), (counts_any, counts_ref), (k_any, k_ref),
                (v_any, v_ref), (cot_any, cot_ref), (w_any, w_ref),
            )
        )
    ]
    for load in loads:
        load.start()

    def copy(slot, source, landing, target):
        return remote(source, landing, send_sem.at[slot], recv_sem.at[slot], target)

    def columns(group):
        return pl.ds(pl.multiple_of(group * width, width), width)

    send_cot = copy(0, cot_any, cots.at[0], to_peer)
    send_cot_far = copy(1, cot_far, cots.at[1], to_peer)
    send_part_far = copy(2, part_out.at[0], part_in.at[0], to_peer)
    send_part_peer = copy(3, part_out.at[1], part_in.at[1], to_peer)
    sent = [send_cot, send_cot_far, send_part_far, send_part_peer]
    if inside:
        fetch_cot = copy(4, cot_any, cot_far, to_far)
        send_far = copy(5, far_out, far_in, to_far)
        sent += [fetch_cot, send_far]

    loads[0].wait()
    lane_head = lax.broadcasted_iota(jnp.int32, (1, width), 1) // HD
    q_scaled = q_ref[...] * jnp.asarray(HD**-0.5, BF)
    for head in range(heads):
        mask = jnp.where(lane_head == head, 1.0, 0.0).astype(BF)
        q_stack[head * rows : (head + 1) * rows, :] = q_scaled * mask
    v_t[:, rows:] = mate_v[...].T
    for load in loads[1:5]:
        load.wait()
    mate_k[...] = choose(partner_ref, k_direct, k_relayed)
    k_t[:, :rows] = k_ref[...].T
    k_t[:, rows:] = mate_k[...].T
    v_t[:, :rows] = v_ref[...].T
    key_row = lax.broadcasted_iota(jnp.int32, (rows, rows), 0)
    own_valid = key_row < counts_ref[b]
    mate_valid = key_row < counts_ref[partner_ref[b]]

    def head_rows(head):
        return pl.ds(pl.multiple_of(head * rows, rows), rows)

    def forward(head, carry):
        own = jnp.where(own_valid, dot_nt(k_ref[...], q_stack[head_rows(head), :]), MASKED)
        other = jnp.where(mate_valid, dot_nt(mate_k[...], q_stack[head_rows(head), :]), MASKED)
        top = jnp.maximum(
            jnp.max(own, axis=0, keepdims=True), jnp.max(other, axis=0, keepdims=True)
        )
        own = jnp.exp(own - top)
        other = jnp.exp(other - top)
        total = jnp.sum(own, axis=0, keepdims=True) + jnp.sum(other, axis=0, keepdims=True)
        inverse = 1.0 / total
        own = own * inverse
        other = other * inverse
        probs[head, :rows, :] = own
        probs[head, rows:, :] = other
        probs_bf[:rows, head_rows(head)] = own.astype(BF)
        probs_bf[rows:, head_rows(head)] = other.astype(BF)
        lanes = pl.ds(pl.multiple_of(head * HD, HD), HD)
        attn_t[lanes, :] = dot(v_t[lanes, :], probs_bf[:, head_rows(head)]).astype(BF)
        return carry

    if inside:
        lax.fori_loop(0, heads // 2, forward, 0, unroll=2)
        pl.semaphore_wait(barrier, 2)
        fetch_cot.start()
        send_cot.start()
        lax.fori_loop(heads // 2, heads, forward, 0, unroll=2)
    else:
        pl.semaphore_wait(barrier, 1)
        send_cot.start()
        send_cot_far.start()
        lax.fori_loop(0, heads, forward, 0, unroll=2)

    loads[6].wait()
    attention = attn_t[...].T
    part_out[0] = dot(attention, w_ref[:, columns(far_peer)]).astype(BF)
    send_part_far.start()
    part_far[...] = dot(attention, w_ref[:, columns(far)])
    part_out[1] = dot(attention, w_ref[:, columns(peer)]).astype(BF)
    send_part_peer.start()
    send_part_far.wait_recv()
    far_out[...] = (part_far[...] + part_in[0].astype(F32)).astype(BF)
    if inside:
        send_far.start()
    part_own[...] = dot(attention, w_ref[:, columns(h)])
    loads[5].wait()
    g_sum[...] = dot_nt(cot_ref[...], w_ref[:, columns(h)])
    send_cot.wait_recv()
    g_sum[...] += dot_nt(cots[0], w_ref[:, columns(peer)])
    send_part_peer.wait_recv()
    part_own[...] += part_in[1].astype(F32)

    if inside:
        fetch_cot.wait_recv()
        send_cot_far.start()
    g_sum[...] += dot_nt(cot_far[...], w_ref[:, columns(far)])
    send_cot_far.wait_recv()
    grad_attention = (g_sum[...] + dot_nt(cots[1], w_ref[:, columns(far_peer)])).astype(BF)
    for head in range(heads):
        mask = jnp.where(lane_head == head, 1.0, 0.0).astype(BF)
        g_stack[head * rows : (head + 1) * rows, :] = grad_attention * mask
    products = grad_attention.T.astype(F32) * attn_t[...].astype(F32)
    delta[...] = jnp.sum(products.reshape(heads, HD, rows), axis=1)

    def backward(head, carry):
        row_delta = delta[pl.ds(head, 1), :]
        for half, values in enumerate((v_ref, mate_v)):
            keys = slice(half * rows, (half + 1) * rows)
            grad_probs = dot_nt(values[...], g_stack[head_rows(head), :])
            grads = probs[head, keys, :] * (grad_probs - row_delta)
            grads_bf[keys, head_rows(head)] = grads.astype(BF)
        lanes = pl.ds(pl.multiple_of(head * HD, HD), HD)
        grads = dot(k_t[lanes, :], grads_bf[:, head_rows(head)])
        dq_t[lanes, :] = (grads * HD**-0.5).astype(BF)
        return carry

    lax.fori_loop(0, heads, backward, 0, unroll=2)
    dq_ref[...] = dq_t[...].T
    dv_cross[...] = dot(probs_bf[rows:, :], g_stack[...]).astype(BF)
    dk_cross[...] = dot(grads_bf[rows:, :], q_stack[...]).astype(BF)
    dv_own[...] = dot(probs_bf[:rows, :], g_stack[...])
    dk_own[...] = dot(grads_bf[:rows, :], q_stack[...])
    if inside:
        send_far.wait_recv()
    for done in sent:
        done.wait_send()


def attend(inside, *operands):
    queries, counts, partner = operands[0], operands[8], operands[9]
    rows, width = queries.shape
    heads = width // HD
    narrow = jax.ShapeDtypeStruct((rows, width), BF)
    wide = jax.ShapeDtypeStruct((rows, width), F32)
    vmem = pl.BlockSpec(memory_space=pltpu.VMEM)
    anywhere = pl.BlockSpec(memory_space=pl.ANY)
    block = pltpu.VMEM((rows, width), BF)
    scratch = [
        block,
        block,
        block,
        block,
        pltpu.VMEM(operands[7].shape, BF),
        pltpu.SMEM(counts.shape, counts.dtype),
        pltpu.SMEM(partner.shape, partner.dtype),
        block,
        pltpu.VMEM((2, rows, width), BF),
        pltpu.VMEM((heads * rows, width), BF),
        pltpu.VMEM((heads * rows, width), BF),
        pltpu.VMEM((width, 2 * rows), BF),
        pltpu.VMEM((width, 2 * rows), BF),
        pltpu.VMEM((heads, 2 * rows, rows), F32),
        pltpu.VMEM((2 * rows, heads * rows), BF),
        pltpu.VMEM((2 * rows, heads * rows), BF),
        pltpu.VMEM((width, rows), BF),
        pltpu.VMEM((width, rows), BF),
        pltpu.VMEM((heads, rows), F32),
        pltpu.VMEM((rows, width), F32),
        pltpu.VMEM((rows, width), F32),
        pltpu.VMEM((2, rows, width), BF),
        pltpu.VMEM((2, rows, width), BF),
        pltpu.SemaphoreType.DMA((7,)),
        pltpu.SemaphoreType.DMA((6,)),
        pltpu.SemaphoreType.DMA((6,)),
    ] + [block] * (2 * inside)
    in_specs = [anywhere] * 3 + [vmem] * 3 + [anywhere] * 4 + [vmem] * (not inside)
    taken, given = len(in_specs), 7

    def body(*refs):
        kernel(inside, refs[:taken], refs[taken : taken + given], refs[taken + given :])

    return pl.pallas_call(
        body,
        out_shape=(wide, narrow, narrow, wide, wide, narrow, narrow),
        in_specs=in_specs,
        out_specs=(vmem,) * given,
        scratch_shapes=scratch,
        compiler_params=pltpu.CompilerParams(
            collective_id=int(inside), has_side_effects=True, vmem_limit_bytes=20 << 20
        ),
        cost_estimate=pl.CostEstimate(
            flops=600_000_000, bytes_accessed=3 << 20, transcendentals=524288
        ),
    )(*operands)


def finish_kernel(
    part_own, far_in, dq, dk_own, dv_own, dk_direct, dk_relayed, dv_in, partner_any,
    lo_out, dq_out, dk_out, dv_out, lo, dk, dv, partner, sems,
):
    load = pltpu.make_async_copy(partner_any, partner, sems.at[0])
    load.start()
    stores = [
        pltpu.make_async_copy(source, target, sems.at[1 + i])
        for i, (source, target) in enumerate(((dq, dq_out), (lo, lo_out), (dv, dv_out), (dk, dk_out)))
    ]
    stores[0].start()
    lo[...] = (part_own[...] + far_in[...].astype(F32)).astype(BF)
    stores[1].start()
    dv[...] = (dv_own[...] + dv_in[...].astype(F32)).astype(BF)
    stores[2].start()
    load.wait()
    dk[...] = (dk_own[...] + choose(partner, dk_direct, dk_relayed).astype(F32)).astype(BF)
    stores[3].start()
    for store in stores:
        store.wait()


def finish(part_own, far_in, dq, dk_own, dv_own, returned, partner):
    vmem = pl.BlockSpec(memory_space=pltpu.VMEM)
    anywhere = pl.BlockSpec(memory_space=pl.ANY)
    return pl.pallas_call(
        finish_kernel,
        out_shape=(jax.ShapeDtypeStruct(dq.shape, BF),) * 4,
        in_specs=[vmem] * 8 + [anywhere],
        out_specs=(anywhere,) * 4,
        scratch_shapes=[pltpu.VMEM(dq.shape, BF)] * 3
        + [pltpu.SMEM(partner.shape, partner.dtype), pltpu.SemaphoreType.DMA((5,))],
        compiler_params=pltpu.CompilerParams(vmem_limit_bytes=4 << 20),
    )(part_own, far_in, dq, dk_own, dv_own, *returned, partner)


PIECES = 4


def near(pair):
    return pair // 2 % 4 == 0


def per_device(queries, key_states, value_states, cotangent, out_weight, partner, counts):
    pair = partner[0] // 2
    everything = range(partner.shape[0] // 2)
    near_pairs = [p for p in everything if near(p)]
    long_pairs = [p for p in everything if not near(p)]

    def stay(queries, key_states, value_states, cotangent, out_weight, partner, counts):
        which = pair // 8 * 2 + pair % 2
        *mates, cotangent_far = swap_any(
            near_pairs, which, (key_states, value_states, cotangent), partner
        )
        part_own, far_out, dq, dk_own, dv_own, dk_cross, dv_cross = attend(
            False, queries, key_states, value_states, *mates, cotangent, out_weight, counts,
            partner, cotangent_far,
        )
        *returned, far_in = swap_any(near_pairs, which, (dk_cross, dv_cross, far_out), partner)
        return finish(part_own, far_in, dq, dk_own, dv_own, returned, partner)

    def cross(queries, key_states, value_states, cotangent, out_weight, partner, counts):
        which = (pair // 8 * 3 + pair // 2 % 4 - 1) * 2 + pair % 2
        mates = swap_any(long_pairs, which, (key_states, value_states), partner)
        part_own, far_in, dq, dk_own, dv_own, dk_cross, dv_cross = attend(
            True, queries, key_states, value_states, *mates, cotangent, out_weight, counts, partner
        )
        returned = swap_any(long_pairs, which, (dk_cross, dv_cross), partner)
        return finish(part_own, far_in, dq, dk_own, dv_own, returned, partner)

    operands = queries, key_states, value_states, cotangent, out_weight, partner, counts
    if not long_pairs:
        return stay(*operands)
    return lax.cond(near(pair), stay, cross, *operands)


def solution(mesh):
    return jax.shard_map(
        per_device,
        mesh=mesh,
        in_specs=(
            P("seq", "head"), P("seq", "head"), P("seq", "head"), P("seq", "head"),
            P("head", None), P(), P(),
        ),
        out_specs=(P("seq", "head"),) * 4,
        check_vma=False,
    )
```

time: 52.3 us -> 54.1 us (1.034)
  the two profiles are of different devices: /device:TPU:32 before, /device:TPU:1 now
where the time goes in v2:
time: 54.1 us; the launch traced here: 53.9 us
  Pallas kernels  51 us (94%)
  local copies, waits for them, and re-layouts  1.31 us (2%)
  between operations  1.03 us (2%)
  loops' own time  0.56 us (1%)
    pallas_call x2, Pallas kernels, swap(): pl.pallas_call(body, out_shape=shapes, in_specs=[anywhere] * taken, out_s...  29.4 us
    pallas_call x1, Pallas kernels, attend(): pl.pallas_call(body, out_shape=(wide, narrow, narrow, wide, wide, narrow,...  20.4 us
    unnamed x4, local copies, waits for them, and re-layouts  1.3 us
    pallas_call x1, Pallas kernels, finish(): pl.pallas_call(finish_kernel, out_shape=(jax.ShapeDtypeStruct(dq.shape, B...  1.29 us

profile of v2, /device:TPU:1, one launch (start us, length us, event | category | flops | bytes accessed | tf_op | source)
XLA Modules:
  0.0 53.9 jit_solution(9751915967072120174)
XLA Ops:
  0.6 0.0 copy-start.1
  0.6 0.6 %copy-done.1 = s32[64]{0:T(128)S(1)} copy-done((s32[64]{0:T(128)S(1)}, s32[64]{0:T(128)}, u32[]{:S(2)}) %copy-start.1) | copy-done | bytes 280
  1.5 0.0 copy-start.6
  1.5 0.6 %copy-done.6 = s32[64]{0:T(128)S(1)} copy-done((s32[64]{0:T(128)S(1)}, s32[64]{0:T(128)}, u32[]{:S(2)}) %copy-start.6) | copy-done | bytes 280
  2.1 51.6 %conditional.5 = ((bf16[256,256]{1,0:T(8,128)(2,1)}, bf16[256,256]{1,0:T(8,128)(2,1)}, bf16[256,256]{1,0:T(8,128)(2,1)}, bf16[256,256]{1,0:T(8,128)(2,1)})) conditional(s32[]{:T(128)} %convert_element_type.3, (s32[]{:T(128)}, bf16[256,256]{1,0:T(8,128)(2,1)}, bf16[256,256]{1,0:T(8,128)(2,1)}, s32[64]{0:T(128)S(1)}, bf16[256,256]{1,0:T(8,128)(2,1)}, ...), branch_computations={%region_0.49_spmd, %region_49.66_spmd} | conditional | flops 600000064 | bytes 6292087 | solution.py:442
  2.1 0.0 copy-start
  2.1 0.0 copy-start.2
  2.1 0.0 copy-start.4
  2.2 15.1 %conditional = ((bf16[256,256]{1,0:T(8,128)(2,1)S(1)}, bf16[256,256]{1,0:T(8,128)(2,1)S(1)}, bf16[256,256]{1,0:T(8,128)(2,1)S(1)})) conditional(s32[]{:T(128)} %clamp.4, (bf16[256,256]{1,0:T(8,128)(2,1)}, bf16[256,256]{1,0:T(8,128)(2,1)}, s32[64]{0:T(128)S(1)}) %tuple.138, (bf16[256,256]{1,0:T(8,128)(2,1)}, ...), branch_computations={%region_1.1_spmd, %region_2.2_spmd, %region_3.3_spmd, %region_4.4_... | conditional | bytes 8 | solution.py:134
  2.2 14.9 %branch_13_fun.2 = (bf16[256,256]{1,0:T(8,128)(2,1)S(1)}, bf16[256,256]{1,0:T(8,128)(2,1)S(1)}, bf16[256,256]{1,0:T(8,128)(2,1)S(1)}) custom-call(bf16[256,256]{1,0:T(8,128)(2,1)} %get-tuple-element.487.refs_0_, bf16[256,256]{1,0:T(8,128)(2,1)} %get-tuple-element.488.refs_1_, s32[64]{0:T(128)S(1)} %get-tuple-element.489.refs_2_), custom_call_target="tpu_custom_call" | custom-call | tf_op jit(solution)/shard_map/cond/branch_0_fun/cond/branch_13_fun/pallas_call | solution.py:114
  17.3 0.0 copy-done
  17.3 0.0 copy-done.2
  17.3 0.0 copy-done.4
  17.3 20.4 %branch_0_fun.8 = (f32[256,256]{1,0:T(8,128)S(1)}, bf16[256,256]{1,0:T(8,128)(2,1)S(1)}, bf16[256,256]{1,0:T(8,128)(2,1)S(1)}, f32[256,256]{1,0:T(8,128)S(1)}, f...) custom-call(bf16[256,256]{1,0:T(8,128)(2,1)S(1)} %copy-done.4, ...), custom_call_target="tpu_custom_call" | custom-call | flops 600000000 | bytes 3145728 | tf_op jit(solution)/shard_map/cond/branch_0_fun/pallas_call | solution.py:354
  37.7 14.5 %conditional.1 = ((bf16[256,256]{1,0:T(8,128)(2,1)S(1)}, bf16[256,256]{1,0:T(8,128)(2,1)S(1)}, bf16[256,256]{1,0:T(8,128)(2,1)S(1)})) conditional(s32[]{:T(128)} %clamp.4, (bf16[256,256]{1,0:T(8,128)(2,1)S(1)}, bf16[256,256]{1,0:T(8,128)(2,1)S(1)}, s32[64]{0:T(128)S(1)}) %tuple.162, (bf16[256,256]{1,0:T(8,128)(2,1)S(1)}, ...), branch_computations={%region_25.25_spmd, %region_26.26_spmd, %region_27.27_spmd, %regio... | conditional | bytes 8 | solution.py:134
  37.7 14.5 %branch_13_fun.3 = (bf16[256,256]{1,0:T(8,128)(2,1)S(1)}, bf16[256,256]{1,0:T(8,128)(2,1)S(1)}, bf16[256,256]{1,0:T(8,128)(2,1)S(1)}) custom-call(bf16[256,256]{1,0:T(8,128)(2,1)S(1)} %get-tuple-element.559.refs_0_, bf16[256,256]{1,0:T(8,128)(2,1)S(1)} %get-tuple-element.560.refs_1_, s32[64]{0:T(128)S(1)} %get-tuple-element.561.refs_2_), custom_call_target="tpu_custom_call" | custom-call | tf_op jit(solution)/shard_map/cond/branch_0_fun/cond/branch_13_fun/pallas_call | solution.py:114
  52.2 1.3 %branch_0_fun.9 = (bf16[256,256]{1,0:T(8,128)(2,1)}, bf16[256,256]{1,0:T(8,128)(2,1)}, bf16[256,256]{1,0:T(8,128)(2,1)}, bf16[256,256]{1,0:T(8,128)(2,1)}) custom-call(f32[256,256]{1,0:T(8,128)S(1)} %get-tuple-element.603.part_own, bf16[256,256]{1,0:T(8,128)(2,1)S(1)} %get-tuple-element.604.far_in, bf16[256,256]{1,0:T(8,128)(2,1)S(1)} %get-tuple-element.605.dq, ...), custom_call_target="tpu_custom_call" | custom-call | tf_op jit(solution)/shard_map/cond/branch_0_fun/pallas_call | solution.py:394
Async XLA Ops:
  0.6 0.7 %copy-start.1 = (s32[64]{0:T(128)S(1)}, s32[64]{0:T(128)}, u32[]{:S(2)}) copy-start(s32[64]{0:T(128)} %param.78) | copy-start | bytes 772
  1.5 0.7 %copy-start.6 = (s32[64]{0:T(128)S(1)}, s32[64]{0:T(128)}, u32[]{:S(2)}) copy-start(s32[64]{0:T(128)} %param.79) | copy-start | bytes 772
  2.1 15.1 %copy-start = (bf16[256,256]{1,0:T(8,128)(2,1)S(1)}, bf16[256,256]{1,0:T(8,128)(2,1)}, u32[]{:S(2)}) copy-start(bf16[256,256]{1,0:T(8,128)(2,1)} %get-tuple-element.600.refs_6_) | copy-start | bytes 393220 | tf_op jit(solution)/shard_map/cond
  2.1 15.1 %copy-start.2 = (bf16[256,1024]{1,0:T(8,128)(2,1)S(1)}, bf16[256,1024]{1,0:T(8,128)(2,1)}, u32[]{:S(2)}) copy-start(bf16[256,1024]{1,0:T(8,128)(2,1)} %get-tuple-element.601.refs_7_) | copy-start | bytes 1572868 | tf_op jit(solution)/shard_map/cond
  2.1 15.1 %copy-start.4 = (bf16[256,256]{1,0:T(8,128)(2,1)S(1)}, bf16[256,256]{1,0:T(8,128)(2,1)}, u32[]{:S(2)}) copy-start(bf16[256,256]{1,0:T(8,128)(2,1)} %get-tuple-element.592.refs_0_) | copy-start | bytes 393220 | tf_op jit(solution)/shard_map/cond

commit v3 on v2

--- a/solution.py
+++ b/solution.py
@@ -73,17 +73,15 @@
     sent_c = [remote(c_ref[0], c_in[0], c_sem.at[0], c_sem.at[1], far)] if c_ref else []
     for copy in sent_c:
         copy.start()
-    for copy in side_b:
-        copy.start()
     if not base:
-        for copy in relay_a:
+        for copy in side_b + relay_a:
             copy.start()
         for copy in side_b + relay_a + sent_c:
             copy.wait()
         return
     direct_a = pieces(a_ref, a_in, a_send, a_recv, mate)
     picked_b = pieces(b_pick, b_in, b_send, b_recv, mate)
-    for copy in direct_a:
+    for copy in direct_a + side_b:
         copy.start()
     load_b.wait()
     load_partner.wait()
@@ -135,7 +133,7 @@
 
 
 def is_relayed(partner_ref):
-    offset = partner_ref[0]
+    offset = partner_ref[0] % partner_ref.shape[0]
     return (offset + offset // 2) % 2 == 1
 
 
@@ -145,16 +143,16 @@
 
 def kernel(inside, inputs, outputs, scratch):
     if inside:
-        q_any, k_any, v_any, k_direct, k_relayed, mate_v, cot_any, w_any, counts_any, partner_any = inputs
+        q_any, k_any, v_any, k_direct, k_relayed, mate_v, cot_any, w_any, partner_any = inputs
         part_own, far_in, dq_ref, dk_own, dv_own, dk_cross, dv_cross = outputs
     else:
         (
-            q_any, k_any, v_any, k_direct, k_relayed, mate_v, cot_any, w_any, counts_any, partner_any,
+            q_any, k_any, v_any, k_direct, k_relayed, mate_v, cot_any, w_any, partner_any,
             cot_far,
         ) = inputs
         part_own, far_out, dq_ref, dk_own, dv_own, dk_cross, dv_cross = outputs
     (
-        q_ref, k_ref, v_ref, cot_ref, w_ref, counts_ref, partner_ref, mate_k, cots, q_stack, g_stack, k_t, v_t, probs, probs_bf,
+        q_ref, k_ref, v_ref, cot_ref, w_ref, partner_ref, mate_k, cots, q_stack, g_stack, k_t, v_t, probs, probs_bf,
         grads_bf, attn_t, dq_t, delta, g_sum, part_far, part_out, part_in, load_sem, send_sem, recv_sem,
         *spare,
     ) = scratch
@@ -177,8 +175,8 @@
         pltpu.make_async_copy(source, landing, load_sem.at[i])
         for i, (source, landing) in enumerate(
             (
-                (q_any, q_ref), (partner_any, partner_ref), (counts_any, counts_ref), (k_any, k_ref),
-                (v_any, v_ref), (cot_any, cot_ref), (w_any, w_ref),
+                (q_any, q_ref), (partner_any, partner_ref), (k_any, k_ref), (v_any, v_ref),
+                (cot_any, cot_ref), (w_any, w_ref),
             )
         )
     ]
@@ -208,15 +206,16 @@
         mask = jnp.where(lane_head == head, 1.0, 0.0).astype(BF)
         q_stack[head * rows : (head + 1) * rows, :] = q_scaled * mask
     v_t[:, rows:] = mate_v[...].T
-    for load in loads[1:5]:
+    for load in loads[1:4]:
         load.wait()
     mate_k[...] = choose(partner_ref, k_direct, k_relayed)
     k_t[:, :rows] = k_ref[...].T
     k_t[:, rows:] = mate_k[...].T
     v_t[:, :rows] = v_ref[...].T
     key_row = lax.broadcasted_iota(jnp.int32, (rows, rows), 0)
-    own_valid = key_row < counts_ref[b]
-    mate_valid = key_row < counts_ref[partner_ref[b]]
+    blocks = partner_ref.shape[0]
+    own_valid = key_row < partner_ref[b] // blocks
+    mate_valid = key_row < partner_ref[partner_ref[b] % blocks] // blocks
 
     def head_rows(head):
         return pl.ds(pl.multiple_of(head * rows, rows), rows)
@@ -253,7 +252,7 @@
         send_cot_far.start()
         lax.fori_loop(0, heads, forward, 0, unroll=2)
 
-    loads[6].wait()
+    loads[5].wait()
     attention = attn_t[...].T
     part_out[0] = dot(attention, w_ref[:, columns(far_peer)]).astype(BF)
     send_part_far.start()
@@ -265,7 +264,7 @@
     if inside:
         send_far.start()
     part_own[...] = dot(attention, w_ref[:, columns(h)])
-    loads[5].wait()
+    loads[4].wait()
     g_sum[...] = dot_nt(cot_ref[...], w_ref[:, columns(h)])
     send_cot.wait_recv()
     g_sum[...] += dot_nt(cots[0], w_ref[:, columns(peer)])
@@ -309,7 +308,7 @@
 
 
 def attend(inside, *operands):
-    queries, counts, partner = operands[0], operands[8], operands[9]
+    queries, partner = operands[0], operands[8]
     rows, width = queries.shape
     heads = width // HD
     narrow = jax.ShapeDtypeStruct((rows, width), BF)
@@ -323,7 +322,6 @@
         block,
         block,
         pltpu.VMEM(operands[7].shape, BF),
-        pltpu.SMEM(counts.shape, counts.dtype),
         pltpu.SMEM(partner.shape, partner.dtype),
         block,
         pltpu.VMEM((2, rows, width), BF),
@@ -341,11 +339,11 @@
         pltpu.VMEM((rows, width), F32),
         pltpu.VMEM((2, rows, width), BF),
         pltpu.VMEM((2, rows, width), BF),
-        pltpu.SemaphoreType.DMA((7,)),
+        pltpu.SemaphoreType.DMA((6,)),
         pltpu.SemaphoreType.DMA((6,)),
         pltpu.SemaphoreType.DMA((6,)),
     ] + [block] * (2 * inside)
-    in_specs = [anywhere] * 3 + [vmem] * 3 + [anywhere] * 4 + [vmem] * (not inside)
+    in_specs = [anywhere] * 3 + [vmem] * 3 + [anywhere] * 3 + [vmem] * (not inside)
     taken, given = len(in_specs), 7
 
     def body(*refs):
@@ -402,7 +400,7 @@
     )(part_own, far_in, dq, dk_own, dv_own, *returned, partner)
 
 
-PIECES = 4
+PIECES = 2
 
 
 def near(pair):
@@ -410,33 +408,35 @@
 
 
 def per_device(queries, key_states, value_states, cotangent, out_weight, partner, counts):
-    pair = partner[0] // 2
+    blocks = partner.shape[0]
+    partner = partner + blocks * counts
+    pair = partner[0] % blocks // 2
     everything = range(partner.shape[0] // 2)
     near_pairs = [p for p in everything if near(p)]
     long_pairs = [p for p in everything if not near(p)]
 
-    def stay(queries, key_states, value_states, cotangent, out_weight, partner, counts):
+    def stay(queries, key_states, value_states, cotangent, out_weight, partner):
         which = pair // 8 * 2 + pair % 2
         *mates, cotangent_far = swap_any(
             near_pairs, which, (key_states, value_states, cotangent), partner
         )
         part_own, far_out, dq, dk_own, dv_own, dk_cross, dv_cross = attend(
-            False, queries, key_states, value_states, *mates, cotangent, out_weight, counts,
-            partner, cotangent_far,
+            False, queries, key_states, value_states, *mates, cotangent, out_weight, partner,
+            cotangent_far,
         )
         *returned, far_in = swap_any(near_pairs, which, (dk_cross, dv_cross, far_out), partner)
         return finish(part_own, far_in, dq, dk_own, dv_own, returned, partner)
 
-    def cross(queries, key_states, value_states, cotangent, out_weight, partner, counts):
+    def cross(queries, key_states, value_states, cotangent, out_weight, partner):
         which = (pair // 8 * 3 + pair // 2 % 4 - 1) * 2 + pair % 2
         mates = swap_any(long_pairs, which, (key_states, value_states), partner)
         part_own, far_in, dq, dk_own, dv_own, dk_cross, dv_cross = attend(
-            True, queries, key_states, value_states, *mates, cotangent, out_weight, counts, partner
+            True, queries, key_states, value_states, *mates, cotangent, out_weight, partner
         )
         returned = swap_any(long_pairs, which, (dk_cross, dv_cross), partner)
         return finish(part_own, far_in, dq, dk_own, dv_own, returned, partner)
 
-    operands = queries, key_states, value_states, cotangent, out_weight, partner, counts
+    operands = queries, key_states, value_states, cotangent, out_weight, partner
     if not long_pairs:
         return stay(*operands)
     return lax.cond(near(pair), stay, cross, *operands)

time: 54.1 us -> 43.5 us (0.80)
  the two profiles are of different devices: /device:TPU:1 before, /device:TPU:8 now
where the time goes in v3:
time: 43.5 us; the launch traced here: 43.4 us
  Pallas kernels  41 us (94%)
  between operations  1 us (2%)
  other arithmetic  0.68 us (2%)
  loops' own time  0.68 us (2%)
    pallas_call x2, Pallas kernels, swap(): pl.pallas_call(body, out_shape=shapes, in_specs=[anywhere] * taken, out_s...  20.4 us
    pallas_call x1, Pallas kernels, attend(): pl.pallas_call(body, out_shape=(wide, narrow, narrow, wide, wide, narrow,...  19.4 us
    pallas_call x1, Pallas kernels, finish(): pl.pallas_call(finish_kernel, out_shape=(jax.ShapeDtypeStruct(dq.shape, B...  1.29 us

profile of v3, /device:TPU:8, one launch (start us, length us, event | category | flops | bytes accessed | tf_op | source)
XLA Modules:
  0.0 43.4 jit_solution(12415108217032904954)
XLA Ops:
  0.6 0.7 %multiply_add_fusion = s32[64]{0:T(128)S(1)} fusion(s32[64]{0:T(128)} %param.78, s32[64]{0:T(128)} %param.79), kind=kLoop, calls=%fused_computation | loop fusion | flops 128 | bytes 768 | tf_op jit(solution)/shard_map/add | solution.py:412
  1.5 41.7 %conditional.5 = ((bf16[256,256]{1,0:T(8,128)(2,1)}, bf16[256,256]{1,0:T(8,128)(2,1)}, bf16[256,256]{1,0:T(8,128)(2,1)}, bf16[256,256]{1,0:T(8,128)(2,1)})) conditional(s32[]{:T(128)} %convert_element_type.3, (s32[]{:T(128)}, bf16[256,256]{1,0:T(8,128)(2,1)}, bf16[256,256]{1,0:T(8,128)(2,1)}, s32[64]{0:T(128)S(1)}, bf16[256,256]{1,0:T(8,128)(2,1)}, ...), branch_computations={%region_0.49_spmd, %region_49.66_spmd} | conditional | flops 600000064 | bytes 6292087 | solution.py:442
  1.6 0.0 copy-start
  1.6 0.0 copy-start.1
  1.6 0.0 copy-start.3
  1.6 10.7 %conditional = ((bf16[256,256]{1,0:T(8,128)(2,1)S(1)}, bf16[256,256]{1,0:T(8,128)(2,1)S(1)}, bf16[256,256]{1,0:T(8,128)(2,1)S(1)})) conditional(s32[]{:T(128)} %clamp.4, (bf16[256,256]{1,0:T(8,128)(2,1)}, bf16[256,256]{1,0:T(8,128)(2,1)}, s32[64]{0:T(128)S(1)}) %tuple.138, (bf16[256,256]{1,0:T(8,128)(2,1)}, ...), branch_computations={%region_1.1_spmd, %region_2.2_spmd, %region_3.3_spmd, %region_4.4_... | conditional | bytes 8 | solution.py:132
  1.6 10.7 %branch_0_fun.6 = (bf16[256,256]{1,0:T(8,128)(2,1)S(1)}, bf16[256,256]{1,0:T(8,128)(2,1)S(1)}, bf16[256,256]{1,0:T(8,128)(2,1)S(1)}) custom-call(bf16[256,256]{1,0:T(8,128)(2,1)} %get-tuple-element.444.refs_0_, bf16[256,256]{1,0:T(8,128)(2,1)} %get-tuple-element.445.refs_1_, s32[64]{0:T(128)S(1)} %get-tuple-element.446.refs_2_), custom_call_target="tpu_custom_call" | custom-call | tf_op jit(solution)/shard_map/cond/branch_0_fun/cond/branch_0_fun/pallas_call | solution.py:112
  12.3 0.0 copy-done
  12.3 0.0 copy-done.1
  12.4 0.0 copy-done.3
  12.4 19.4 %branch_0_fun.8 = (f32[256,256]{1,0:T(8,128)S(1)}, bf16[256,256]{1,0:T(8,128)(2,1)S(1)}, bf16[256,256]{1,0:T(8,128)(2,1)S(1)}, f32[256,256]{1,0:T(8,128)S(1)}, f...) custom-call(bf16[256,256]{1,0:T(8,128)(2,1)S(1)} %copy-done.3, ...), custom_call_target="tpu_custom_call" | custom-call | flops 600000000 | bytes 3145728 | tf_op jit(solution)/shard_map/cond/branch_0_fun/pallas_call | solution.py:352
  31.7 10.0 %conditional.1 = ((bf16[256,256]{1,0:T(8,128)(2,1)S(1)}, bf16[256,256]{1,0:T(8,128)(2,1)S(1)}, bf16[256,256]{1,0:T(8,128)(2,1)S(1)})) conditional(s32[]{:T(128)} %clamp.4, (bf16[256,256]{1,0:T(8,128)(2,1)S(1)}, bf16[256,256]{1,0:T(8,128)(2,1)S(1)}, s32[64]{0:T(128)S(1)}) %tuple.162, (bf16[256,256]{1,0:T(8,128)(2,1)S(1)}, ...), branch_computations={%region_25.25_spmd, %region_26.26_spmd, %region_27.27_spmd, %regio... | conditional | bytes 8 | solution.py:132
  31.8 9.7 %branch_0_fun.7 = (bf16[256,256]{1,0:T(8,128)(2,1)S(1)}, bf16[256,256]{1,0:T(8,128)(2,1)S(1)}, bf16[256,256]{1,0:T(8,128)(2,1)S(1)}) custom-call(bf16[256,256]{1,0:T(8,128)(2,1)S(1)} %get-tuple-element.516.refs_0_, bf16[256,256]{1,0:T(8,128)(2,1)S(1)} %get-tuple-element.517.refs_1_, s32[64]{0:T(128)S(1)} %get-tuple-element.518.refs_2_), custom_call_target="tpu_custom_call" | custom-call | tf_op jit(solution)/shard_map/cond/branch_0_fun/cond/branch_0_fun/pallas_call | solution.py:112
  41.7 1.3 %branch_0_fun.9 = (bf16[256,256]{1,0:T(8,128)(2,1)}, bf16[256,256]{1,0:T(8,128)(2,1)}, bf16[256,256]{1,0:T(8,128)(2,1)}, bf16[256,256]{1,0:T(8,128)(2,1)}) custom-call(f32[256,256]{1,0:T(8,128)S(1)} %get-tuple-element.598.part_own, bf16[256,256]{1,0:T(8,128)(2,1)S(1)} %get-tuple-element.599.far_in, bf16[256,256]{1,0:T(8,128)(2,1)S(1)} %get-tuple-element.600.dq, ...), custom_call_target="tpu_custom_call" | custom-call | tf_op jit(solution)/shard_map/cond/branch_0_fun/pallas_call | solution.py:392
Async XLA Ops:
  1.6 10.8 %copy-start = (bf16[256,256]{1,0:T(8,128)(2,1)S(1)}, bf16[256,256]{1,0:T(8,128)(2,1)}, u32[]{:S(2)}) copy-start(bf16[256,256]{1,0:T(8,128)(2,1)} %get-tuple-element.596.refs_6_) | copy-start | bytes 393220 | tf_op jit(solution)/shard_map/cond
  1.6 10.8 %copy-start.1 = (bf16[256,1024]{1,0:T(8,128)(2,1)S(1)}, bf16[256,1024]{1,0:T(8,128)(2,1)}, u32[]{:S(2)}) copy-start(bf16[256,1024]{1,0:T(8,128)(2,1)} %get-tuple-element.597.refs_7_) | copy-start | bytes 1572868 | tf_op jit(solution)/shard_map/cond
  1.6 10.8 %copy-start.3 = (bf16[256,256]{1,0:T(8,128)(2,1)S(1)}, bf16[256,256]{1,0:T(8,128)(2,1)}, u32[]{:S(2)}) copy-start(bf16[256,256]{1,0:T(8,128)(2,1)} %get-tuple-element.588.refs_0_) | copy-start | bytes 393220 | tf_op jit(solution)/shard_map/cond
